TPU v7x, 32 devices: a whole 2x2x4 slice. The times are simulated.
32 devices in a mesh: groups: 2 (over x), replica: 16 (over z, y, core).
Axes of the slice: x: 2, y: 2, z: 4, core: 2. Of those that a mesh axis runs over, the one named last changes fastest.
Arguments:
- page_table: int32 [32, 64], P(('groups', 'replica')), parts along dimension 0, may hold values from 0 to 1023, as said below
- prefix_len: int32 [32], P(('groups', 'replica')), parts along dimension 0, may hold values from 64 to 512, as said below
- page_store: bfloat16 [2048, 8, 2048], P(('groups', 'replica')), parts along dimension 0, may hold values from -16 to 16
- cand_query: bfloat16 [32, 800, 2048], P(('groups', 'replica')), parts along dimension 0, may hold values from -16 to 16
- cand_kv: bfloat16 [32, 800, 2048], P(('groups', 'replica')), parts along dimension 0, may hold values from -6 to 6
Outputs:
- attended: bfloat16 [32, 800, 2048], P(('groups', 'replica')), parts along dimension 0
There are 2 independent parts, one for each index of `groups`. A program takes and returns all parts, laid end to end along the dimension named above; each array names one. Nothing has to cross between parts.
Inputs may be any that keep to these rules, and one draw needn't show every extreme that they name: `page_table`: entry [q, k] = 64 * d + s names slot s of device d, which holds page k of query q's prefix. Every slot is named exactly once. No device holds more than 16 pages of one query, and every query has exactly 16 pages on some device. `prefix_len`: positions from the prefix length on are unused. Some query has 64 tokens and some has 512.
All inputs are finite; a program needn't handle non-finite values.
Results may differ from a plain program's by a relative error of at most 0.007.
Values may be sent and summed in bfloat16 or wider, within the bound.
A program may use at most 128 MiB of HBM per device.

v0:
```python
import jax
import jax.numpy as jnp
from jax import lax
from jax.sharding import PartitionSpec as P

HD = 256
QH = 8
KH = 4
CLEN = 200


def rope_turn(values, positions):
    head_width = values.shape[-1]
    half_width = head_width // 2
    pair_index = jnp.arange(half_width, dtype=jnp.float32)
    inverse = jnp.power(jnp.float32(10000.0), pair_index * (-2.0 / head_width))
    angles = positions.astype(jnp.float32)[:, None] * inverse[None, :]
    cosine = jnp.cos(angles)[:, None, :]
    sine_table = jnp.sin(angles)[:, None, :]
    leading = values[..., :half_width]
    trailing = values[..., half_width:]
    return jnp.concatenate(
        [leading * cosine - trailing * sine_table, trailing * cosine + leading * sine_table],
        axis=-1,
    )


def pick_slots(tables, chosen, capacity, held):
    counted = jnp.cumsum(chosen.astype(jnp.int32), axis=1) - 1
    picked = chosen[:, None, :] & (counted[:, None, :] == jnp.arange(capacity)[None, :, None])
    return jnp.sum(jnp.where(picked, (tables % held)[:, None, :], 0), axis=2)


def attend_local(rotated, prefix_keys, prefix_values, own_keys, own_values, length, cand_count):
    scale = HD ** (-0.5)
    grouped = rotated.reshape(cand_count, CLEN, KH, QH // KH, HD)
    prefix_scores = (
        jnp.einsum("ctkgd,pkd->ctkgp", grouped, prefix_keys, preferred_element_type=jnp.float32)
        * scale
    )
    prefix_scores = 50.0 * jnp.tanh(prefix_scores / 50.0)
    live = jnp.arange(prefix_keys.shape[0]) < length
    own_grouped = own_keys.reshape(cand_count, CLEN, KH, HD)
    own_scores = (
        jnp.einsum("ctkgd,cskd->ctkgs", grouped, own_grouped, preferred_element_type=jnp.float32)
        * scale
    )
    own_scores = 50.0 * jnp.tanh(own_scores / 50.0)
    causal = jnp.arange(CLEN)[:, None] >= jnp.arange(CLEN)[None, :]
    prefix_exp = jnp.where(live, jnp.exp(prefix_scores), 0.0)
    own_exp = jnp.where(causal[None, :, None, None, :], jnp.exp(own_scores), 0.0)
    denominator = jnp.sum(prefix_exp, axis=-1) + jnp.sum(own_exp, axis=-1)
    prefix_weights = prefix_exp.astype(jnp.bfloat16)
    own_weights = own_exp.astype(jnp.bfloat16)
    own_vals = own_values.reshape(cand_count, CLEN, KH, HD)
    total = jnp.einsum(
        "ctkgp,pkd->ctkgd", prefix_weights, prefix_values, preferred_element_type=jnp.float32
    )
    total = total + jnp.einsum(
        "ctkgs,cskd->ctkgd", own_weights, own_vals, preferred_element_type=jnp.float32
    )
    result = total / denominator[..., None]
    return result.reshape(cand_count * CLEN, QH * HD).astype(jnp.bfloat16)


def body(page_table, prefix_len, page_store, cand_query, cand_kv):
    peers = lax.axis_size("replica")
    my_index = lax.axis_index("replica")
    held = page_store.shape[0]
    capacity = max(2, 4 * held // peers)
    table = page_table[0]
    source = table // held
    page_ids = jnp.arange(held)
    same_source = (source[:, None] == source[None, :]) & (page_ids[None, :] < page_ids[:, None])
    rank_here = jnp.sum(same_source.astype(jnp.int32), axis=1)
    every_table = lax.all_gather(page_table, "replica", axis=0, tiled=True)
    send_slot = pick_slots(every_table, every_table // held == my_index, capacity, held)
    rows = cand_query.shape[1]
    cand_count = rows // CLEN
    length = prefix_len[0]
    positions = length + jnp.arange(rows, dtype=jnp.int32) % CLEN
    rotated = rope_turn(cand_query[0].reshape(rows, QH, HD).astype(jnp.float32), positions).astype(
        jnp.bfloat16
    )
    own = cand_kv[0].reshape(rows, 2, KH, HD)
    own_keys = rope_turn(own[:, 0].astype(jnp.float32), positions).astype(jnp.bfloat16)
    prefix_tokens = held * page_store.shape[1]
    outgoing = page_store[send_slot]
    arrived = lax.all_to_all(outgoing, "replica", split_axis=0, concat_axis=0, tiled=True)
    prefix = arrived[source, rank_here].reshape(prefix_tokens, 2, KH, HD)
    prefix_keys = prefix[:, 0]
    prefix_values = prefix[:, 1]
    result = attend_local(
        rotated, prefix_keys, prefix_values, own_keys, own[:, 1], length, cand_count
    )
    return result[None]


def solution(mesh):
    return jax.shard_map(
        body,
        mesh=mesh,
        in_specs=(
            P(("groups", "replica"), None),
            P(("groups", "replica")),
            P(("groups", "replica"), None, None),
            P(("groups", "replica"), None, None),
            P(("groups", "replica"), None, None),
        ),
        out_specs=P(("groups", "replica"), None, None),
        check_vma=False,
    )
```

profile of v0, /device:TPU:15, one launch (start us, length us, event | category | flops | bytes accessed | tf_op | source)
XLA Modules:
  0.0 257.2 jit_solution(3706529410822205312)
XLA Ops:
  0.0 0.0 copy-start
  0.0 15.7 %all-gather = s32[16,1,64]{2,1,0:T(1,128)S(1)} all-gather(s32[1,1,64]{2,1,0:T(1,128)} %bitcast.111), channel_id=1, replica_groups=mesh['groups'=2,'replica'=16] {'replica'}, dimensions={0}, use_global_device_ids=true | all-gather | bytes 4352 | tf_op jit(solution)/shard_map/all_gather | solution.py:76
  15.8 0.2 reduce_window_sum.11
  16.0 0.3 select_reduce_fusion
  16.4 0.1 reshape.237
  16.4 0.0 copy-done
  16.5 8.4 %gather_fusion = bf16[256,8,2048]{2,1,0:T(8,128)(2,1)} fusion(bf16[64,8,2048]{2,1,0:T(8,128)(2,1)S(1)} %copy-done, s32[1024]{0:T(1024)S(1)} %pad_clamp_fusion), kind=kCustom, calls=%fused_computation | custom fusion | bytes 16778240 | tf_op jit(solution)/shard_map/gather | solution.py:88
  24.8 11.3 %all-to-all-start = ((bf16[16,16,8,2048]{3,2,1,0:T(8,128)(2,1)}), bf16[16,16,8,2048]{3,2,1,0:T(8,128)(2,1)}, u32[]{:S(2)}, u32[]{:S(2)}) async-start(bf16[16,16,8,2048]{3,2,1,0:T(8,128)(2,1)} %bitcast.99), calls=%async_computation | async-start | bytes 16777216 | tf_op jit(solution)/shard_map/all_to_all | solution.py:89
  36.8 5.5 %copy.98 = f32[100,8,8,256]{3,2,1,0:T(8,128)} copy(bf16[100,8,8,256]{3,1,2,0:T(8,128)(2,1)} %bitcast.105) | data formatting | bytes 9830400
  42.2 7.8 %reshape_squeeze.7 = bf16[800,2,4,256]{3,2,1,0:T(4,128)(2,1)} reshape(bf16[1,800,2048]{2,1,0:T(8,128)(2,1)} %param.9) | data formatting | bytes 6553600 | tf_op jit(solution)/shard_map/reshape;squeeze | solution.py:85
  50.1 1.5 multiply_cosine_fusion
  51.6 0.0 slice-start
  51.6 3.1 %fusion.42 = (bf16[800,1,4,256]{3,2,1,0:T(4,128)(2,1)S(1)}, f32[800,4,256]{2,1,0:T(4,128)S(1)}) fusion(bf16[800,2,4,256]{3,2,1,0:T(4,128)(2,1)} %reshape_squeeze.7), kind=kLoop, calls=%fused_computation.93 | loop fusion | flops 819200 | bytes 8192000 | tf_op jit(solution)/shard_map/slice | solution.py:94
  54.7 0.0 slice-start.1
  54.7 1.0 subtract_convert_fusion.1
  55.7 0.0 copy-start.5
  55.7 0.1 copy.76
  55.8 0.1 copy.75
  55.9 1.4 copy.78
  57.3 0.0 copy-done.5
  57.4 0.2 convert_reduce_fusion
  57.6 0.0 slice-done
  57.6 0.0 slice-done.1
  57.6 1.0 add_convert_fusion
  58.6 0.3 copy_dynamic-update-slice_fusion.1
  58.9 0.5 copy_dynamic-update-slice_fusion
  59.4 0.0 copy-start.3
  59.4 1.7 copy-done.3
  61.1 3.7 %fusion.8 = (bf16[4,200,4,2,200]{1,4,3,2,0:T(8,128)(2,1)}, f32[4,200,4,2]{1,3,2,0:T(2,128)S(1)}) fusion(pred[200,200]{0,1:T(8,128)(4,1)S(1)} %iota_compare_fusion, bf16[4,200,4,2,256]{4,1,3,0,2:T(8,128)(2,1)S(1)} %copy_dynamic-update-slice_fusion, bf16[4,200,4,128]{3,1,2,0:T(8,128)(2,1)S(1)} %copy.76, bf16[4,200,4,128]{3,1,2,0:T(8,128)(2,1)S(1)} %copy.75), kind=kOutput, calls=%fused_computation.15 | convolution fusion | flops 665030400 | bytes 7540800 | tf_op jit(solution)/shard_map/ctkgd,cskd->ctkgs/dot_general | solution.py:45
  64.9 153.6 %all-to-all-done = bf16[16,16,8,2048]{3,2,1,0:T(8,128)(2,1)} async-done(((bf16[16,16,8,2048]{3,2,1,0:T(8,128)(2,1)}), bf16[16,16,8,2048]{3,2,1,0:T(8,128)(2,1)}, u32[]{:S(2)}, u32[]{:S(2)}) %all-to-all-start) | async-done | bytes 8388640 | tf_op jit(solution)/shard_map/all_to_all | solution.py:89
  218.5 5.4 %gather_fusion.1 = bf16[64,8,2048]{2,1,0:T(8,128)(2,1)} fusion(bf16[16,16,8,2048]{3,2,1,0:T(8,128)(2,1)} %all-to-all-done, s32[64]{0:T(128)S(1)} %fusion.35), kind=kCustom, calls=%fused_computation.1 | custom fusion | bytes 4194816 | tf_op jit(solution)/shard_map/gather | solution.py:90
  223.9 3.3 %reshape.232 = bf16[512,2,4,256]{3,2,1,0:T(4,128)(2,1)S(1)} reshape(bf16[64,8,2048]{2,1,0:T(8,128)(2,1)} %gather_fusion.1) | data formatting | bytes 4194304 | tf_op jit(solution)/shard_map/reshape | solution.py:90
  227.3 0.0 copy-start.4
  227.3 0.7 fusion.43
  228.0 1.2 copy-done.4
  229.2 4.8 %bitcast_reduce_fusion = (f32[4,200,4,2]{1,3,0,2:T(2,128)S(1)}, f32[4,512,4,200,2]{1,3,4,2,0:T(8,128)S(1)}) fusion(pred[512]{0:T(512)(128)(4,1)S(1)} %iota_compare_fusion.3, bf16[4,200,4,2,256]{4,1,3,0,2:T(8,128)(2,1)S(1)} %copy-done.4, bf16[512,1,4,256]{3,2,1,0:T(4,128)(2,1)S(1)} %get-tuple-element.16), kind=kOutput, calls=%fused_computation.2 | convolution fusion | flops 1690822400 | bytes 17458688 | tf_op jit(solution)/shard_map/ctkgd,pkd->ctkgp/dot_general | solution.py:38
  234.0 0.0 copy-start.2
  234.0 5.7 %fusion = f32[4,256,4,200,2]{1,3,4,2,0:T(8,128)} fusion(f32[4,512,4,200,2]{1,3,4,2,0:T(8,128)S(1)} %get-tuple-element.20, pred[512]{0:T(512)(128)(4,1)S(1)} %iota_compare_fusion.3, bf16[512,1,4,256]{3,2,1,0:T(4,128)(2,1)S(1)} %get-tuple-element.15), kind=kOutput, calls=%fused_computation.5 | convolution fusion | flops 1690828800 | bytes 20709888 | tf_op jit(solution)/shard_map/ctkgp,pkd->ctkgd/dot_general | solution.py:56
  239.8 0.0 copy-done.2
  239.8 5.0 %fusion.2 = bf16[4,200,4,2,256]{4,1,3,0,2:T(8,128)(2,1)S(1)} fusion(f32[4,256,4,200,2]{1,3,4,2,0:T(8,128)} %fusion, f32[4,200,4,2]{1,3,0,2:T(2,128)S(1)} %copy_add_fusion, bf16[4,200,4,256,1]{3,1,4,0,2:T(8,128)(2,1)S(1)} %bitcast.108, bf16[4,200,4,2,200]{1,4,3,2,0:T(8,128)(2,1)} %get-tuple-element.9), kind=kOutput, calls=%fused_computation.8 | convolution fusion | flops 660275200 | bytes 14054400 | tf_op jit(solution)/shard_map/ctkgs,cskd->ctkgd/dot_general | solution.py:59
  244.8 0.0 copy-start.1
  244.8 4.2 %copy.81 = bf16[4,200,4,2,256]{4,3,2,1,0:T(2,128)(2,1)} copy(bf16[4,200,4,2,256]{4,1,3,0,2:T(8,128)(2,1)S(1)} %fusion.2) | data formatting | bytes 6553600 | tf_op jit(solution)/shard_map/convert_element_type | solution.py:63
  249.0 8.2 %convert_element_type.59 = bf16[1,800,2048]{2,1,0:T(8,128)(2,1)} reshape(bf16[4,200,4,2,256]{4,3,2,1,0:T(2,128)(2,1)} %copy.81) | data formatting | bytes 6553600 | tf_op jit(solution)/shard_map/convert_element_type | solution.py:63
  257.2 0.0 copy-done.1
  (13 shorter events, 0.1 us)
Async XLA Ops:
  0.0 16.4 %copy-start = (bf16[64,8,2048]{2,1,0:T(8,128)(2,1)S(1)}, bf16[64,8,2048]{2,1,0:T(8,128)(2,1)}, u32[]{:S(2)}) copy-start(bf16[64,8,2048]{2,1,0:T(8,128)(2,1)} %param.7) | copy-start | bytes 6291460
  24.8 193.7 %all-to-all-start = ((bf16[16,16,8,2048]{3,2,1,0:T(8,128)(2,1)}), bf16[16,16,8,2048]{3,2,1,0:T(8,128)(2,1)}, u32[]{:S(2)}, u32[]{:S(2)}) async-start(bf16[16,16,8,2048]{3,2,1,0:T(8,128)(2,1)} %bitcast.99), calls=%async_computation | async-start | bytes 16777216 | tf_op jit(solution)/shard_map/all_to_all | solution.py:89
  51.6 6.0 %slice-start = ((s8[6553600]{0:T(1024)(128)(4,1)}), s8[2359296]{0:T(1024)(128)(4,1)S(1)}, s32[]{:S(2)}) async-start(s8[6553600]{0:T(1024)(128)(4,1)} %bitcast.100), calls=%async_computation.1 | async-start | bytes 4718592
  54.7 2.9 %slice-start.1 = ((s8[6553600]{0:T(1024)(128)(4,1)}), s8[4194304]{0:T(1024)(128)(4,1)S(1)}, s32[]{:S(2)}) async-start(s8[6553600]{0:T(1024)(128)(4,1)} %bitcast.100), calls=%async_computation.2 | async-start | bytes 8388608
  55.7 1.7 copy-start.5
  59.4 1.7 copy-start.3
  227.3 1.9 copy-start.4
  234.0 5.7 %copy-start.2 = (bf16[800,1,4,256]{3,0,2,1:T(8,128)(2,1)S(1)}, bf16[800,1,4,256]{3,0,2,1:T(8,128)(2,1)}, u32[]{:S(2)}) copy-start(bf16[800,1,4,256]{3,0,2,1:T(8,128)(2,1)} %copy.78) | copy-start | bytes 4915204
  244.8 12.4 %copy-start.1 = (bf16[64,8,2048]{2,1,0:T(8,128)(2,1)S(1)}, bf16[64,8,2048]{2,1,0:T(8,128)(2,1)}, u32[]{:S(2)}) copy-start(bf16[64,8,2048]{2,1,0:T(8,128)(2,1)} %param.7) | copy-start | bytes 6291460
where the time goes:
time: 258 us; the launch traced here: 257 us
  waiting for transfers between devices  154 us (60%)
  local copies, waits for them, and re-layouts  48.9 us (19%)
  matrix products  19.3 us (7%)
  blocking collectives  15.7 us (6%)
  starting transfers between devices  11.3 us (4%)
  other arithmetic  7.43 us (3%)
    all_to_all x1, waiting for transfers between devices, body(): lax.all_to_all(outgoing, 'replica', split_axis=0, concat_axis=0, tiled=True)  154 us
    all_gather x1, blocking collectives, body(): every_table = lax.all_gather(page_table, 'replica', axis=0, tiled=True)  15.7 us
    convert_element_type x2, local copies, waits for them, and re-layouts, attend_local(): return result.reshape(cand_count * CLEN, QH * HD).astype(jnp.bfloat16)  12.4 us
    all_to_all x1, starting transfers between devices, body(): lax.all_to_all(outgoing, 'replica', split_axis=0, concat_axis=0, tiled=True)  11.3 us
    unnamed x18, local copies, waits for them, and re-layouts  8.66 us
    gather x1, local copies, waits for them, and re-layouts, body(): outgoing = page_store[send_slot]  8.38 us
    another operation x1, local copies, waits for them, and re-layouts, body(): own = cand_kv[0].reshape(rows, 2, KH, HD)  7.84 us
    dot_general x1, matrix products, attend_local(): jnp.einsum('ctkgp,pkd->ctkgd', prefix_weights, prefix_values, preferred_e...  5.69 us
  transfers between devices with their start and end apart: 1, of which 1 were waited for; matrix products, arithmetic and copies ran while one was open for 10% of the time, Pallas kernels for 0%

commit v1 on v0

v1 whole, which is shorter than its diff:
```python
import functools
import math

import jax
import jax.numpy as jnp
from jax import lax
from jax.experimental import pallas as pl
from jax.experimental.pallas import tpu as pltpu
from jax.sharding import PartitionSpec as P

HD = 256
QH = 8
KH = 4
CLEN = 200
LANES = 128
MESH = pl.DeviceIdType.MESH


def pick_slots(tables, chosen, capacity, held):
    counted = jnp.cumsum(chosen.astype(jnp.int32), axis=1) - 1
    picked = chosen[:, None, :] & (counted[:, None, :] == jnp.arange(capacity)[None, :, None])
    return jnp.sum(jnp.where(picked, (tables % held)[:, None, :], 0), axis=2)


def padded_exchange(page_table, page_store):
    peers = lax.axis_size("replica")
    my_index = lax.axis_index("replica")
    held = page_store.shape[0]
    capacity = max(2, 4 * held // peers)
    table = page_table[0]
    source = (table // held) % peers
    page_ids = jnp.arange(held)
    same_source = (source[:, None] == source[None, :]) & (page_ids[None, :] < page_ids[:, None])
    rank_here = jnp.sum(same_source.astype(jnp.int32), axis=1)
    every_table = lax.all_gather(page_table, "replica", axis=0, tiled=True)
    mine = (every_table // held) % peers == my_index
    send_slot = pick_slots(every_table, mine, capacity, held)
    outgoing = page_store[send_slot]
    arrived = lax.all_to_all(outgoing, "replica", split_axis=0, concat_axis=0, tiled=True)
    return arrived[source, rank_here].reshape(held * page_store.shape[1], page_store.shape[2])


def route_kernel(groups, peers, held, share, table_ref, out_ref, tables, send_sem, recv_sem):
    group = lax.axis_index("groups")
    me = lax.axis_index("replica")
    total = groups * peers
    flat = group * peers + me
    barrier = pltpu.get_barrier_semaphore()

    def where_is(step):
        other = lax.rem(flat + step, total)
        return other, (lax.div(other, peers), lax.rem(other, peers))

    def greet(step, carry):
        pl.semaphore_signal(barrier, inc=1, device_id=where_is(step)[1], device_id_type=MESH)
        return carry

    lax.fori_loop(1, total, greet, 0)
    tables[pl.ds(flat, 1)] = table_ref[...][None]
    pl.semaphore_wait(barrier, total - 1)

    def outgoing(step):
        return pltpu.make_async_remote_copy(
            src_ref=table_ref,
            dst_ref=tables.at[flat],
            send_sem=send_sem.at[step],
            recv_sem=recv_sem.at[flat],
            device_id=where_is(step)[1],
            device_id_type=MESH,
        )

    def send(step, carry):
        outgoing(step).start()
        return carry

    def finish(step, carry):
        other, place = where_is(step)
        pltpu.make_async_remote_copy(
            src_ref=table_ref,
            dst_ref=tables.at[other],
            send_sem=send_sem.at[step],
            recv_sem=recv_sem.at[other],
            device_id=place,
            device_id_type=MESH,
        ).wait()
        return carry

    lax.fori_loop(1, total, send, 0)
    lax.fori_loop(1, total, finish, 0)

    every = tables[:, 0, :]
    shape = (total, LANES)
    row = lax.broadcasted_iota(jnp.int32, shape, 0)
    lane = lax.broadcasted_iota(jnp.int32, shape, 1)
    valid = lane < held
    query = lax.rem(row, peers)
    owner = jnp.where(valid, lax.rem(lax.div(every, held), peers), -1)
    slot = lax.rem(every, held)
    before = (
        lax.broadcasted_iota(jnp.int32, (LANES, LANES), 0)
        < lax.broadcasted_iota(jnp.int32, (LANES, LANES), 1)
    ).astype(jnp.float32)
    left = lax.broadcasted_iota(jnp.int32, (total, total), 0)
    right = lax.broadcasted_iota(jnp.int32, (total, total), 1)
    together = lax.div(left, peers) == lax.div(right, peers)
    rank = jnp.zeros(shape, jnp.float32)
    for device in range(peers):
        here = (owner == device).astype(jnp.float32)
        along = jnp.dot(here, before, preferred_element_type=jnp.float32)
        nearer = lax.rem(right + (peers - device), peers) < lax.rem(left + (peers - device), peers)
        earlier = (together & nearer).astype(jnp.float32)
        above = jnp.dot(earlier, here, preferred_element_type=jnp.float32)
        above = jnp.sum(above, axis=1, keepdims=True)
        rank = rank + here * (along + above)
    rank = rank.astype(jnp.int32)
    middle = jnp.where(valid, lax.rem(rank, peers), -1)
    layer = lax.div(rank, peers)
    place = jnp.zeros(shape, jnp.float32)
    for device in range(peers):
        here = (middle == device).astype(jnp.float32)
        along = jnp.dot(here, before, preferred_element_type=jnp.float32)
        place = place + here * along
    most = jnp.max(jnp.max(place, axis=1, keepdims=True), axis=0, keepdims=True)
    place = place.astype(jnp.int32)

    mine = lax.div(row, peers) == group
    first_key = jnp.where(mine & (owner == me), middle * share + layer, -1)
    second_key = jnp.where(mine & (middle == me), query * share + place, -1)
    second_value = owner * share + layer
    spots = lax.broadcasted_iota(jnp.int32, (held, LANES), 0)
    first = jnp.zeros((held, LANES), jnp.int32)
    second = jnp.zeros((held, LANES), jnp.int32)
    for index in range(total):
        cut = slice(index, index + 1)
        first = first + jnp.where(spots == first_key[cut], slot[cut], 0)
        second = second + jnp.where(spots == second_key[cut], second_value[cut], 0)
    ones = jnp.ones((8, LANES), jnp.float32)
    turn = (((1,), (1,)), ((), ()))
    first_row = lax.dot_general(ones, first.astype(jnp.float32), turn, preferred_element_type=jnp.float32)
    second_row = lax.dot_general(ones, second.astype(jnp.float32), turn, preferred_element_type=jnp.float32)
    last_row = jnp.sum(jnp.where((row == flat) & valid, middle * share + place, 0), axis=0, keepdims=True)
    out_ref[...] = jnp.zeros(out_ref.shape, jnp.int32)
    out_ref[0:1, 0:held] = first_row[0:1].astype(jnp.int32)
    out_ref[1:2, 0:held] = second_row[0:1].astype(jnp.int32)
    out_ref[2:3, :] = last_row
    out_ref[3:4, :] = jnp.broadcast_to(most.astype(jnp.int32), (1, LANES))


def find_routes(page_table, groups, peers, held, share):
    padded = jnp.broadcast_to(jnp.pad(page_table, ((0, 0), (0, LANES - held))), (8, LANES))
    total = groups * peers
    return pl.pallas_call(
        functools.partial(route_kernel, groups, peers, held, share),
        out_shape=jax.ShapeDtypeStruct((8, LANES), jnp.int32),
        in_specs=[pl.BlockSpec(memory_space=pltpu.VMEM)],
        out_specs=pl.BlockSpec(memory_space=pltpu.VMEM),
        scratch_shapes=[
            pltpu.VMEM((total, 8, LANES), jnp.int32),
            pltpu.SemaphoreType.DMA((total,)),
            pltpu.SemaphoreType.DMA((total,)),
        ],
        compiler_params=pltpu.CompilerParams(collective_id=0, has_side_effects=True),
        name="routes",
    )(padded)


def hops_kernel(
    peers, held, share, route_ref, store_ref, out_ref, *scratch
):
    out1, in1, out2, in2 = scratch[0:2], scratch[2:4], scratch[4:6], scratch[6:8]
    s1, r1, s2, r2 = scratch[8:12]
    group = lax.axis_index("groups")
    me = lax.axis_index("replica")
    half = store_ref.shape[2] // 2
    barrier = pltpu.get_barrier_semaphore()

    def peer(step):
        return lax.rem(me + step, peers)

    def greet(step, carry):
        pl.semaphore_signal(barrier, inc=1, device_id=(group, peer(step)), device_id_type=MESH)
        return carry

    lax.fori_loop(1, peers, greet, 0)

    def block(index):
        return pl.ds(index * share, share)

    def copy(part, step, source, target, send_sem, recv_sem, who):
        other = peer(step)
        return pltpu.make_async_remote_copy(
            src_ref=source[part].at[block(other)],
            dst_ref=target[part].at[block(who)],
            send_sem=send_sem.at[part, step],
            recv_sem=recv_sem.at[part, who],
            device_id=(group, other),
            device_id_type=MESH,
        )

    def start_all(part, source, target, send_sem, recv_sem):
        def one(step, carry):
            copy(part, step, source, target, send_sem, recv_sem, me).start()
            return carry

        lax.fori_loop(1, peers, one, 0)
        target[part][block(me)] = source[part][block(me)]

    def await_all(part, source, target, send_sem, recv_sem):
        def one(step, carry):
            copy(part, step, source, target, send_sem, recv_sem, peer(step)).wait_recv()
            return carry

        lax.fori_loop(1, peers, one, 0)

    def drain(part, source, target, send_sem, recv_sem):
        def one(step, carry):
            copy(part, step, source, target, send_sem, recv_sem, me).wait_send()
            return carry

        lax.fori_loop(1, peers, one, 0)

    hop1 = (out1, in1, s1, r1)
    hop2 = (out2, in2, s2, r2)
    for part in range(2):
        columns = slice(part * half, (part + 1) * half)

        def gather(index, carry):
            out1[part][index] = store_ref[route_ref[0, index], :, columns]
            return carry

        lax.fori_loop(0, held, gather, 0)
        if part == 0:
            pl.semaphore_wait(barrier, peers - 1)
        start_all(part, *hop1)
    for part in range(2):
        await_all(part, *hop1)

        def forward(index, carry):
            out2[part][index] = in1[part][route_ref[1, index]]
            return carry

        lax.fori_loop(0, held, forward, 0)
        start_all(part, *hop2)
    for part in range(2):
        columns = slice(part * half, (part + 1) * half)
        await_all(part, *hop2)

        def settle(index, carry):
            upper = in2[part][route_ref[2, 2 * index]].astype(jnp.float32)
            lower = in2[part][route_ref[2, 2 * index + 1]].astype(jnp.float32)
            both = jnp.concatenate([upper, lower], axis=0).astype(out_ref.dtype)
            out_ref[pl.ds(pl.multiple_of(index * 16, 16), 16), columns] = both
            return carry

        lax.fori_loop(0, held // 2, settle, 0)
    for part in range(2):
        drain(part, *hop1)
        drain(part, *hop2)


def two_hops(routes, page_store, peers, held, share):
    page, width = page_store.shape[1:]
    buffer = pltpu.VMEM((held, page, width // 2), page_store.dtype)
    sems = pltpu.SemaphoreType.DMA((2, peers))
    return pl.pallas_call(
        functools.partial(hops_kernel, peers, held, share),
        out_shape=jax.ShapeDtypeStruct((held * page, width), page_store.dtype),
        in_specs=[
            pl.BlockSpec(memory_space=pltpu.SMEM),
            pl.BlockSpec(memory_space=pltpu.VMEM),
        ],
        out_specs=pl.BlockSpec(memory_space=pltpu.VMEM),
        scratch_shapes=[buffer] * 8 + [sems] * 4,
        compiler_params=pltpu.CompilerParams(
            collective_id=1, has_side_effects=True, vmem_limit_bytes=32 * 1024 * 1024
        ),
        name="hops",
    )(routes, page_store)


def attend_kernel(length_ref, cos_ref, sin_ref, q_ref, k_ref, v_ref, pk_ref, pv_ref, o_ref):
    gain = 50.0 * math.log2(math.e)
    shrink = HD ** (-0.5) / 50.0
    half = HD // 2
    heads = QH // KH
    cosine = cos_ref[...]
    sine = sin_ref[...]
    contract = (((1,), (1,)), ((), ()))

    def turn(values):
        leading = values[:, :half]
        trailing = values[:, half:]
        return jnp.concatenate(
            [leading * cosine - trailing * sine, trailing * cosine + leading * sine], axis=1
        )

    tokens = pk_ref.shape[0]
    column = lax.broadcasted_iota(jnp.int32, (1, tokens), 1)
    bias = jnp.where(column < length_ref[0], 0.0, -1e30).astype(jnp.float32)
    causal = lax.broadcasted_iota(jnp.int32, (CLEN, CLEN), 0) >= lax.broadcasted_iota(
        jnp.int32, (CLEN, CLEN), 1
    )
    pk = pk_ref[...]
    pv = pv_ref[...]
    span = 2 * CLEN
    for pair in range(q_ref.shape[0] // span):
        rows = slice(pair * span, (pair + 1) * span)
        queries = q_ref[rows, :].astype(jnp.float32)
        keys = k_ref[rows, :].astype(jnp.float32)
        values = v_ref[rows, :].astype(jnp.float32)
        results = []
        for cand in range(2):
            part = slice(cand * CLEN, (cand + 1) * CLEN)
            own_k = turn(keys[part]).astype(jnp.bfloat16)
            own_v = values[part].astype(jnp.bfloat16)
            row = []
            for head in range(heads):
                rotated = turn(queries[part, head * HD : (head + 1) * HD]).astype(jnp.bfloat16)
                far = lax.dot_general(rotated, pk, contract, preferred_element_type=jnp.float32)
                near = lax.dot_general(rotated, own_k, contract, preferred_element_type=jnp.float32)
                far = jnp.exp2(jnp.tanh(far * shrink) * gain + bias)
                near = jnp.where(causal, jnp.exp2(jnp.tanh(near * shrink) * gain), 0.0)
                total = jnp.sum(far, axis=1, keepdims=True) + jnp.sum(near, axis=1, keepdims=True)
                mixed = jnp.dot(far.astype(jnp.bfloat16), pv, preferred_element_type=jnp.float32)
                mixed = mixed + jnp.dot(
                    near.astype(jnp.bfloat16), own_v, preferred_element_type=jnp.float32
                )
                row.append(mixed / total)
            results.append(row)
        for head in range(heads):
            both = jnp.concatenate([results[0][head], results[1][head]], axis=0)
            o_ref[rows, head * HD : (head + 1) * HD] = both.astype(o_ref.dtype)


def attend(length, cosine, sine, queries, paired, prefix):
    rows = queries.shape[0]
    tokens = prefix.shape[0]
    wide = (QH // KH) * HD
    whole = lambda g: (0, 0)
    return pl.pallas_call(
        attend_kernel,
        grid=(KH,),
        out_shape=jax.ShapeDtypeStruct(queries.shape, queries.dtype),
        in_specs=[
            pl.BlockSpec(memory_space=pltpu.SMEM),
            pl.BlockSpec((CLEN, HD // 2), whole),
            pl.BlockSpec((CLEN, HD // 2), whole),
            pl.BlockSpec((rows, wide), lambda g: (0, g)),
            pl.BlockSpec((rows, HD), lambda g: (0, g)),
            pl.BlockSpec((rows, HD), lambda g: (0, KH + g)),
            pl.BlockSpec((tokens, HD), lambda g: (0, g)),
            pl.BlockSpec((tokens, HD), lambda g: (0, KH + g)),
        ],
        out_specs=pl.BlockSpec((rows, wide), lambda g: (0, g)),
        compiler_params=pltpu.CompilerParams(vmem_limit_bytes=48 * 1024 * 1024),
        name="attend",
    )(length, cosine, sine, queries, paired, paired, prefix, prefix)


def body(page_table, prefix_len, page_store, cand_query, cand_kv):
    groups = lax.axis_size("groups")
    peers = lax.axis_size("replica")
    held = page_store.shape[0]
    share = held // peers
    capacity = max(2, 4 * held // peers)
    length = prefix_len[0]
    positions = length + jnp.arange(CLEN, dtype=jnp.int32)
    pair_index = jnp.arange(HD // 2, dtype=jnp.float32)
    inverse = jnp.power(jnp.float32(10000.0), pair_index * (-2.0 / HD))
    angles = positions.astype(jnp.float32)[:, None] * inverse[None, :]
    cosine = jnp.cos(angles)
    sine = jnp.sin(angles)
    if share * peers == held and 2 * share < capacity:
        routes = find_routes(page_table, groups, peers, held, share)
        prefix = lax.cond(
            routes[3, 0] < share,
            lambda: two_hops(routes, page_store, peers, held, share),
            lambda: padded_exchange(page_table, page_store),
        )
    else:
        prefix = padded_exchange(page_table, page_store)
    return attend(prefix_len, cosine, sine, cand_query[0], cand_kv[0], prefix)[None]


def solution(mesh):
    return jax.shard_map(
        body,
        mesh=mesh,
        in_specs=(
            P(("groups", "replica"), None),
            P(("groups", "replica")),
            P(("groups", "replica"), None, None),
            P(("groups", "replica"), None, None),
            P(("groups", "replica"), None, None),
        ),
        out_specs=P(("groups", "replica"), None, None),
        check_vma=False,
    )
```

time: 258 us -> 130 us (0.50)
  waiting for transfers between devices: 154 us -> 0 us
  Pallas kernels: 0 us -> 126 us
  local copies, waits for them, and re-layouts: 48.9 us -> 1.77 us
  matrix products: 19.3 us -> 0 us
  blocking collectives: 15.7 us -> 0 us
  starting transfers between devices: 11.3 us -> 0 us
  other arithmetic: 7.43 us -> 0.45 us
    all_to_all x1 -> x0, waiting for transfers between devices: 154 us -> none  [body(): lax.all_to_all(outgoing, 'replica', split_axis=0, concat_axis=0, tiled=True)]
    pallas_call x0 -> x3, Pallas kernels: none -> 126 us  [the longest x1 101 us: two_hops(): pl.pallas_call(functools.partial(hops_kernel, peers, held, share), out_sh...]
    dot_general x4 -> x0, matrix products: 19.3 us -> none  [the longest x1 5.69 us: attend_local(): jnp.einsum('ctkgp,pkd->ctkgd', prefix_weights, prefix_values, preferred_e...]
    all_gather x1 -> x0, blocking collectives: 15.7 us -> none  [body(): every_table = lax.all_gather(page_table, 'replica', axis=0, tiled=True)]
    gather x2 -> x0, local copies, waits for them, and re-layouts: 13.8 us -> none  [the longest x1 8.38 us: body(): outgoing = page_store[send_slot]]
    convert_element_type x2 -> x0, local copies, waits for them, and re-layouts: 12.4 us -> none  [attend_local(): return result.reshape(cand_count * CLEN, QH * HD).astype(jnp.bfloat16)]
    all_to_all x1 -> x0, starting transfers between devices: 11.3 us -> none  [body(): lax.all_to_all(outgoing, 'replica', split_axis=0, concat_axis=0, tiled=True)]
    unnamed x18 -> x2, local copies, waits for them, and re-layouts: 8.66 us -> 0.01 us
  transfers between devices with their start and end apart: 1 -> 0, of which waited for: 1 -> 0; matrix products, arithmetic and copies ran while one was open for 10% -> 0% of each run, Pallas kernels for 0% -> 0%
where the time goes in v1:
time: 130 us; the launch traced here: 129 us
  Pallas kernels  126 us (97%)
  local copies, waits for them, and re-layouts  1.77 us (1%)
  between operations  1.35 us (1%)
    pallas_call x1, Pallas kernels, two_hops(): pl.pallas_call(functools.partial(hops_kernel, peers, held, share), out_sh...  101 us
    pallas_call x1, Pallas kernels, attend(): pl.pallas_call(attend_kernel, grid=(KH,), out_shape=jax.ShapeDtypeStruct(...  13.4 us
    pallas_call x1, Pallas kernels, find_routes(): pl.pallas_call(functools.partial(route_kernel, groups, peers, held, share...  11.3 us

profile of v1, /device:TPU:15, one launch (start us, length us, event | category | flops | bytes accessed | tf_op | source)
XLA Modules:
  0.0 129.5 jit_solution(11083441053862022343)
XLA Ops:
  0.0 0.7 pad_bitcast_fusion
  0.7 0.6 broadcast_in_dim.15.table_ref
  1.3 11.3 %routes.1 = s32[8,128]{1,0:T(8,128)S(1)} custom-call(s32[8,128]{1,0:T(8,128)} %broadcast_in_dim.15.table_ref), custom_call_target="tpu_custom_call" | custom-call | tf_op jit(solution)/shard_map/routes/pallas_call | solution.py:152
  12.5 0.5 slice.3
  13.7 0.0 copy-start
  13.7 101.2 %conditional.1 = (bf16[512,2048]{1,0:T(8,128)(2,1)}) conditional(s32[]{:T(128)} %bitcast.14, (s32[1,64]{1,0:T(1,128)}, bf16[64,8,2048]{2,1,0:T(8,128)(2,1)}) %tuple.11, (s32[8,128]{1,0:T(8,128)S(1)}, bf16[64,8,2048]{2,1,0:T(8,128)(2,1)}) %tuple.12), branch_computations={%region_0.4_spmd, %region_4.5_spmd} | conditional | flops 198658 | bytes 46200160 | solution.py:375
  13.7 101.2 %hops.1 = bf16[512,2048]{1,0:T(8,128)(2,1)} custom-call(s32[8,128]{1,0:T(8,128)S(1)} %get-tuple-element.18.route_ref, bf16[64,8,2048]{2,1,0:T(8,128)(2,1)} %get-tuple-element.19.store_ref), custom_call_target="tpu_custom_call" | custom-call | tf_op jit(solution)/shard_map/cond/branch_1_fun/hops/pallas_call | solution.py:265
  115.6 0.4 multiply_sine_fusion
  116.0 0.0 copy-done
  116.0 13.4 %attend.1 = bf16[800,2048]{1,0:T(8,128)(2,1)} custom-call(s32[1]{0:T(128)} %copy.9.length_ref, f32[200,128]{1,0:T(8,128)S(1)} %get-tuple-element.25.cos_ref, f32[200,128]{1,0:T(8,128)S(1)} %get-tuple-element.24.sin_ref, bf16[800,2048]{1,0:T(8,128)(2,1)S(1)} %bitcast.46, bf16[800,2048]{1,0:T(8,128)(2,1)} %bitcast.49, bf16[800,2048]{1,0:T(8,128)(2,1)} %bitcast.50, ...), custom_call_target="tpu_custom_call" | custom-call | tf_op jit(solution)/shard_map/attend/pallas_call | solution.py:340
  (2 shorter events, 0.0 us)
Async XLA Ops:
  13.7 102.3 %copy-start = (bf16[1,800,2048]{2,1,0:T(8,128)(2,1)S(1)}, bf16[1,800,2048]{2,1,0:T(8,128)(2,1)}, u32[]{:S(2)}) copy-start(bf16[1,800,2048]{2,1,0:T(8,128)(2,1)} %param.10) | copy-start | bytes 9830404

commit v2 on v1

--- a/solution.py
+++ b/solution.py
@@ -164,14 +164,13 @@
     )(padded)
 
 
-def hops_kernel(
-    peers, held, share, route_ref, store_ref, out_ref, *scratch
+def serve_kernel(
+    peers, held, share, route_ref, length_ref, cos_ref, sin_ref, store_ref, q_ref, kv_ref, o_ref, *scratch
 ):
-    out1, in1, out2, in2 = scratch[0:2], scratch[2:4], scratch[4:6], scratch[6:8]
-    s1, r1, s2, r2 = scratch[8:12]
+    out1, in1, out2, in2 = (scratch[i * KH : (i + 1) * KH] for i in range(4))
+    s1, r1, s2, r2, prefix = scratch[4 * KH :]
     group = lax.axis_index("groups")
     me = lax.axis_index("replica")
-    half = store_ref.shape[2] // 2
     barrier = pltpu.get_barrier_semaphore()
 
     def peer(step):
@@ -221,18 +220,20 @@
 
     hop1 = (out1, in1, s1, r1)
     hop2 = (out2, in2, s2, r2)
-    for part in range(2):
-        columns = slice(part * half, (part + 1) * half)
+    for part in range(KH):
+        key_columns = slice(part * HD, (part + 1) * HD)
+        value_columns = slice((KH + part) * HD, (KH + part + 1) * HD)
 
         def gather(index, carry):
-            out1[part][index] = store_ref[route_ref[0, index], :, columns]
+            out1[part][index, :, 0:HD] = store_ref[route_ref[0, index], :, key_columns]
+            out1[part][index, :, HD:] = store_ref[route_ref[0, index], :, value_columns]
             return carry
 
         lax.fori_loop(0, held, gather, 0)
         if part == 0:
             pl.semaphore_wait(barrier, peers - 1)
         start_all(part, *hop1)
-    for part in range(2):
+    for part in range(KH):
         await_all(part, *hop1)
 
         def forward(index, carry):
@@ -241,44 +242,56 @@
 
         lax.fori_loop(0, held, forward, 0)
         start_all(part, *hop2)
-    for part in range(2):
-        columns = slice(part * half, (part + 1) * half)
+    for part in range(KH):
         await_all(part, *hop2)
 
         def settle(index, carry):
             upper = in2[part][route_ref[2, 2 * index]].astype(jnp.float32)
             lower = in2[part][route_ref[2, 2 * index + 1]].astype(jnp.float32)
-            both = jnp.concatenate([upper, lower], axis=0).astype(out_ref.dtype)
-            out_ref[pl.ds(pl.multiple_of(index * 16, 16), 16), columns] = both
+            both = jnp.concatenate([upper, lower], axis=0).astype(prefix.dtype)
+            prefix[pl.ds(pl.multiple_of(index * 16, 16), 16), :] = both
             return carry
 
         lax.fori_loop(0, held // 2, settle, 0)
-    for part in range(2):
+        wide = (QH // KH) * HD
+        attend_head(
+            length_ref,
+            cos_ref,
+            sin_ref,
+            q_ref.at[:, part * wide : (part + 1) * wide],
+            kv_ref.at[:, part * HD : (part + 1) * HD],
+            kv_ref.at[:, (KH + part) * HD : (KH + part + 1) * HD],
+            prefix[:, 0:HD],
+            prefix[:, HD:],
+            o_ref.at[:, part * wide : (part + 1) * wide],
+        )
+    for part in range(KH):
         drain(part, *hop1)
         drain(part, *hop2)
 
 
-def two_hops(routes, page_store, peers, held, share):
-    page, width = page_store.shape[1:]
-    buffer = pltpu.VMEM((held, page, width // 2), page_store.dtype)
-    sems = pltpu.SemaphoreType.DMA((2, peers))
+def serve(routes, length, cosine, sine, page_store, queries, paired, peers, held, share):
+    page = page_store.shape[1]
+    buffer = pltpu.VMEM((held, page, 2 * HD), page_store.dtype)
+    sems = pltpu.SemaphoreType.DMA((KH, peers))
+    vmem = pl.BlockSpec(memory_space=pltpu.VMEM)
+    smem = pl.BlockSpec(memory_space=pltpu.SMEM)
     return pl.pallas_call(
-        functools.partial(hops_kernel, peers, held, share),
-        out_shape=jax.ShapeDtypeStruct((held * page, width), page_store.dtype),
-        in_specs=[
-            pl.BlockSpec(memory_space=pltpu.SMEM),
-            pl.BlockSpec(memory_space=pltpu.VMEM),
-        ],
-        out_specs=pl.BlockSpec(memory_space=pltpu.VMEM),
-        scratch_shapes=[buffer] * 8 + [sems] * 4,
+        functools.partial(serve_kernel, peers, held, share),
+        out_shape=jax.ShapeDtypeStruct(queries.shape, queries.dtype),
+        in_specs=[smem, smem, vmem, vmem, vmem, vmem, vmem],
+        out_specs=vmem,
+        scratch_shapes=[buffer] * (4 * KH)
+        + [sems] * 4
+        + [pltpu.VMEM((held * page, 2 * HD), page_store.dtype)],
         compiler_params=pltpu.CompilerParams(
-            collective_id=1, has_side_effects=True, vmem_limit_bytes=32 * 1024 * 1024
+            collective_id=1, has_side_effects=True, vmem_limit_bytes=48 * 1024 * 1024
         ),
-        name="hops",
-    )(routes, page_store)
-
-
-def attend_kernel(length_ref, cos_ref, sin_ref, q_ref, k_ref, v_ref, pk_ref, pv_ref, o_ref):
+        name="serve",
+    )(routes, length, cosine, sine, page_store, queries, paired)
+
+
+def attend_head(length_ref, cos_ref, sin_ref, q_ref, k_ref, v_ref, pk, pv, o_ref):
     gain = 50.0 * math.log2(math.e)
     shrink = HD ** (-0.5) / 50.0
     half = HD // 2
@@ -294,17 +307,16 @@
             [leading * cosine - trailing * sine, trailing * cosine + leading * sine], axis=1
         )
 
-    tokens = pk_ref.shape[0]
+    tokens = pk.shape[0]
     column = lax.broadcasted_iota(jnp.int32, (1, tokens), 1)
     bias = jnp.where(column < length_ref[0], 0.0, -1e30).astype(jnp.float32)
     causal = lax.broadcasted_iota(jnp.int32, (CLEN, CLEN), 0) >= lax.broadcasted_iota(
         jnp.int32, (CLEN, CLEN), 1
     )
-    pk = pk_ref[...]
-    pv = pv_ref[...]
     span = 2 * CLEN
-    for pair in range(q_ref.shape[0] // span):
-        rows = slice(pair * span, (pair + 1) * span)
+
+    def one_pair(pair, carry):
+        rows = pl.ds(pl.multiple_of(pair * span, span), span)
         queries = q_ref[rows, :].astype(jnp.float32)
         keys = k_ref[rows, :].astype(jnp.float32)
         values = v_ref[rows, :].astype(jnp.float32)
@@ -330,6 +342,13 @@
         for head in range(heads):
             both = jnp.concatenate([results[0][head], results[1][head]], axis=0)
             o_ref[rows, head * HD : (head + 1) * HD] = both.astype(o_ref.dtype)
+        return carry
+
+    lax.fori_loop(0, q_ref.shape[0] // span, one_pair, 0)
+
+
+def attend_kernel(length_ref, cos_ref, sin_ref, q_ref, k_ref, v_ref, pk_ref, pv_ref, o_ref):
+    attend_head(length_ref, cos_ref, sin_ref, q_ref, k_ref, v_ref, pk_ref[...], pv_ref[...], o_ref)
 
 
 def attend(length, cosine, sine, queries, paired, prefix):
@@ -370,16 +389,22 @@
     angles = positions.astype(jnp.float32)[:, None] * inverse[None, :]
     cosine = jnp.cos(angles)
     sine = jnp.sin(angles)
+    queries = cand_query[0]
+    paired = cand_kv[0]
+
+    def padded():
+        prefix = padded_exchange(page_table, page_store)
+        return attend(prefix_len, cosine, sine, queries, paired, prefix)
+
+    def hopped():
+        return serve(
+            routes, prefix_len, cosine, sine, page_store, queries, paired, peers, held, share
+        )
+
     if share * peers == held and 2 * share < capacity:
         routes = find_routes(page_table, groups, peers, held, share)
-        prefix = lax.cond(
-            routes[3, 0] < share,
-            lambda: two_hops(routes, page_store, peers, held, share),
-            lambda: padded_exchange(page_table, page_store),
-        )
-    else:
-        prefix = padded_exchange(page_table, page_store)
-    return attend(prefix_len, cosine, sine, cand_query[0], cand_kv[0], prefix)[None]
+        return lax.cond(routes[3, 0] < share, hopped, padded)[None]
+    return padded()[None]
 
 
 def solution(mesh):

time: 130 us -> 123 us (0.946)
  Pallas kernels: 126 us -> 117 us
  local copies, waits for them, and re-layouts: 1.77 us -> 3.48 us
    pallas_call x2 -> x1, Pallas kernels: 115 us -> 106 us  [serve(): pl.pallas_call(functools.partial(serve_kernel, peers, held, share), out_s...]
    unnamed x2 -> x1, local copies, waits for them, and re-layouts: 0.01 us -> 1.71 us
where the time goes in v2:
time: 123 us
  Pallas kernels  117 us (95%)
  local copies, waits for them, and re-layouts  3.48 us (3%)
  between operations  1.34 us (1%)
    pallas_call x1, Pallas kernels, serve(): pl.pallas_call(functools.partial(serve_kernel, peers, held, share), out_s...  106 us
    pallas_call x1, Pallas kernels, find_routes(): pl.pallas_call(functools.partial(route_kernel, groups, peers, held, share...  11.3 us

profile of v2, /device:TPU:15, one launch (start us, length us, event | category | flops | bytes accessed | tf_op | source)
XLA Modules:
  0.0 122.6 jit_solution(5643385103492200388)
XLA Ops:
  0.7 0.4 multiply_sine_fusion
  1.1 0.7 pad_bitcast_fusion
  1.8 0.6 broadcast_in_dim.23.table_ref
  2.4 11.3 %routes.1 = s32[8,128]{1,0:T(8,128)S(1)} custom-call(s32[8,128]{1,0:T(8,128)} %broadcast_in_dim.23.table_ref), custom_call_target="tpu_custom_call" | custom-call | tf_op jit(solution)/shard_map/routes/pallas_call | solution.py:152
  13.6 0.5 slice.3
  14.8 106.1 %conditional.1 = (bf16[1,800,2048]{2,1,0:T(8,128)(2,1)S(1)}) conditional(s32[]{:T(128)} %bitcast.13, (s32[1,64]{1,0:T(1,128)}, bf16[64,8,2048]{2,1,0:T(8,128)(2,1)}, s32[1]{0:T(128)}, f32[200,128]{1,0:T(8,128)S(1)}, f32[200,128]{1,0:T(8,128)S(1)}, /*index=5*/bf16[800,2048]{1,0:T(8,128)(2,1)}, bf16[800,2048]{1,0:T(8,128)(2,1)}) %tuple.24, ...), branch_computations={%region_0.4_spmd, %region_4.5_spmd} | conditional | flops 198658 | bytes 46200160 | solution.py:406
  15.0 105.9 %serve.1 = bf16[800,2048]{1,0:T(8,128)(2,1)S(1)} custom-call(s32[8,128]{1,0:T(8,128)S(1)} %get-tuple-element.44.route_ref, s32[1]{0:T(128)} %get-tuple-element.45.length_ref, f32[200,128]{1,0:T(8,128)S(1)} %get-tuple-element.46.cos_ref, f32[200,128]{1,0:T(8,128)S(1)} %get-tuple-element.47.sin_ref, bf16[64,8,2048]{2,1,0:T(8,128)(2,1)} %get-tuple-element.48.store_ref, ...), custom_call_target="tpu_custom_call" | custom-call | tf_op jit(solution)/shard_map/cond/branch_1_fun/serve/pallas_call | solution.py:279
  120.9 1.7 %copy.13 = bf16[1,800,2048]{2,1,0:T(8,128)(2,1)} copy(bf16[1,800,2048]{2,1,0:T(8,128)(2,1)S(1)} %get-tuple-element.51) | data formatting | bytes 6553600
  (2 shorter events, 0.0 us)

commit v3 on v2

--- a/solution.py
+++ b/solution.py
@@ -40,7 +40,13 @@
     return arrived[source, rank_here].reshape(held * page_store.shape[1], page_store.shape[2])
 
 
-def route_kernel(groups, peers, held, share, table_ref, out_ref, tables, send_sem, recv_sem):
+def split(values, size):
+    if size & (size - 1) == 0:
+        return lax.shift_right_logical(values, jnp.int32(size.bit_length() - 1)), values & (size - 1)
+    return lax.div(values, size), lax.rem(values, size)
+
+
+def route_kernel(groups, peers, held, share, row_ref, out_ref, most_ref, table_ref, tables, send_sem, recv_sem):
     group = lax.axis_index("groups")
     me = lax.axis_index("replica")
     total = groups * peers
@@ -56,6 +62,8 @@
         return carry
 
     lax.fori_loop(1, total, greet, 0)
+    table_ref[...] = jnp.zeros(table_ref.shape, jnp.int32)
+    table_ref[0:1, 0:held] = row_ref[...]
     tables[pl.ds(flat, 1)] = table_ref[...][None]
     pl.semaphore_wait(barrier, total - 1)
 
@@ -93,28 +101,34 @@
     row = lax.broadcasted_iota(jnp.int32, shape, 0)
     lane = lax.broadcasted_iota(jnp.int32, shape, 1)
     valid = lane < held
-    query = lax.rem(row, peers)
-    owner = jnp.where(valid, lax.rem(lax.div(every, held), peers), -1)
-    slot = lax.rem(every, held)
+    query = row
+    for lap in range(1, groups):
+        query = jnp.where(row >= lap * peers, row - lap * peers, query)
+    device_of, slot = split(every, held)
+    owner = jnp.where(valid, split(device_of, peers)[1], -1)
     before = (
         lax.broadcasted_iota(jnp.int32, (LANES, LANES), 0)
         < lax.broadcasted_iota(jnp.int32, (LANES, LANES), 1)
     ).astype(jnp.float32)
     left = lax.broadcasted_iota(jnp.int32, (total, total), 0)
     right = lax.broadcasted_iota(jnp.int32, (total, total), 1)
-    together = lax.div(left, peers) == lax.div(right, peers)
+    left_lap, left = split(left, peers)
+    right_lap, right = split(right, peers)
+    together = left_lap == right_lap
     rank = jnp.zeros(shape, jnp.float32)
     for device in range(peers):
         here = (owner == device).astype(jnp.float32)
         along = jnp.dot(here, before, preferred_element_type=jnp.float32)
-        nearer = lax.rem(right + (peers - device), peers) < lax.rem(left + (peers - device), peers)
+        nearer = jnp.where(right < device, right + peers, right) < jnp.where(
+            left < device, left + peers, left
+        )
         earlier = (together & nearer).astype(jnp.float32)
         above = jnp.dot(earlier, here, preferred_element_type=jnp.float32)
         above = jnp.sum(above, axis=1, keepdims=True)
         rank = rank + here * (along + above)
     rank = rank.astype(jnp.int32)
-    middle = jnp.where(valid, lax.rem(rank, peers), -1)
-    layer = lax.div(rank, peers)
+    layer, middle = split(rank, peers)
+    middle = jnp.where(valid, middle, -1)
     place = jnp.zeros(shape, jnp.float32)
     for device in range(peers):
         here = (middle == device).astype(jnp.float32)
@@ -123,7 +137,7 @@
     most = jnp.max(jnp.max(place, axis=1, keepdims=True), axis=0, keepdims=True)
     place = place.astype(jnp.int32)
 
-    mine = lax.div(row, peers) == group
+    mine = (row >= group * peers) & (row < (group + 1) * peers)
     first_key = jnp.where(mine & (owner == me), middle * share + layer, -1)
     second_key = jnp.where(mine & (middle == me), query * share + place, -1)
     second_value = owner * share + layer
@@ -143,25 +157,28 @@
     out_ref[0:1, 0:held] = first_row[0:1].astype(jnp.int32)
     out_ref[1:2, 0:held] = second_row[0:1].astype(jnp.int32)
     out_ref[2:3, :] = last_row
-    out_ref[3:4, :] = jnp.broadcast_to(most.astype(jnp.int32), (1, LANES))
+    most_ref[...] = most.astype(jnp.int32)
 
 
 def find_routes(page_table, groups, peers, held, share):
-    padded = jnp.broadcast_to(jnp.pad(page_table, ((0, 0), (0, LANES - held))), (8, LANES))
     total = groups * peers
     return pl.pallas_call(
         functools.partial(route_kernel, groups, peers, held, share),
-        out_shape=jax.ShapeDtypeStruct((8, LANES), jnp.int32),
+        out_shape=[
+            jax.ShapeDtypeStruct((8, LANES), jnp.int32),
+            jax.ShapeDtypeStruct((1, 1), jnp.int32),
+        ],
         in_specs=[pl.BlockSpec(memory_space=pltpu.VMEM)],
-        out_specs=pl.BlockSpec(memory_space=pltpu.VMEM),
+        out_specs=[pl.BlockSpec(memory_space=pltpu.VMEM)] * 2,
         scratch_shapes=[
+            pltpu.VMEM((8, LANES), jnp.int32),
             pltpu.VMEM((total, 8, LANES), jnp.int32),
             pltpu.SemaphoreType.DMA((total,)),
             pltpu.SemaphoreType.DMA((total,)),
         ],
         compiler_params=pltpu.CompilerParams(collective_id=0, has_side_effects=True),
         name="routes",
-    )(padded)
+    )(page_table)
 
 
 def serve_kernel(
@@ -402,8 +419,8 @@
         )
 
     if share * peers == held and 2 * share < capacity:
-        routes = find_routes(page_table, groups, peers, held, share)
-        return lax.cond(routes[3, 0] < share, hopped, padded)[None]
+        routes, most = find_routes(page_table, groups, peers, held, share)
+        return lax.cond(most[0, 0] < share, hopped, padded)[None]
     return padded()[None]
 
 

time: 123 us -> 121 us (0.984)
  local copies, waits for them, and re-layouts: 3.48 us -> 1.71 us
    broadcast_in_dim x2 -> x0, local copies, waits for them, and re-layouts: 1.26 us -> none  [find_routes(): jnp.broadcast_to(jnp.pad(page_table, ((0, 0), (0, LANES - held))), (8, LA...]
where the time goes in v3:
time: 121 us
  Pallas kernels  118 us (98%)
  local copies, waits for them, and re-layouts  1.71 us (1%)
  between operations  1.32 us (1%)
    pallas_call x1, Pallas kernels, serve(): pl.pallas_call(functools.partial(serve_kernel, peers, held, share), out_s...  106 us
    pallas_call x1, Pallas kernels, find_routes(): pl.pallas_call(functools.partial(route_kernel, groups, peers, held, share...  11.6 us

profile of v3, /device:TPU:15, one launch (start us, length us, event | category | flops | bytes accessed | tf_op | source)
XLA Modules:
  0.0 121.2 jit_solution(12876916315277640392)
XLA Ops:
  0.7 0.4 multiply_sine_fusion
  1.1 11.6 %routes.1 = (s32[8,128]{1,0:T(8,128)S(1)}, s32[1,1]{1,0:T(1,128)}) custom-call(s32[1,64]{1,0:T(1,128)} %row_ref.1), custom_call_target="tpu_custom_call" | custom-call | tf_op jit(solution)/shard_map/routes/pallas_call | solution.py:165
  13.4 106.1 %conditional.1 = (bf16[1,800,2048]{2,1,0:T(8,128)(2,1)S(1)}) conditional(s32[]{:T(128)} %bitcast.12, (s32[1,64]{1,0:T(1,128)}, bf16[64,8,2048]{2,1,0:T(8,128)(2,1)}, s32[1]{0:T(128)}, f32[200,128]{1,0:T(8,128)S(1)}, f32[200,128]{1,0:T(8,128)S(1)}, /*index=5*/bf16[800,2048]{1,0:T(8,128)(2,1)}, bf16[800,2048]{1,0:T(8,128)(2,1)}) %tuple.24, ...), branch_computations={%region_0.4_spmd, %region_4.5_spmd} | conditional | flops 198658 | bytes 46200160 | solution.py:423
  13.6 105.9 %serve.1 = bf16[800,2048]{1,0:T(8,128)(2,1)S(1)} custom-call(s32[8,128]{1,0:T(8,128)S(1)} %get-tuple-element.44.route_ref, s32[1]{0:T(128)} %get-tuple-element.45.length_ref, f32[200,128]{1,0:T(8,128)S(1)} %get-tuple-element.46.cos_ref, f32[200,128]{1,0:T(8,128)S(1)} %get-tuple-element.47.sin_ref, bf16[64,8,2048]{2,1,0:T(8,128)(2,1)} %get-tuple-element.48.store_ref, ...), custom_call_target="tpu_custom_call" | custom-call | tf_op jit(solution)/shard_map/cond/branch_1_fun/serve/pallas_call | solution.py:296
  119.5 1.7 %copy.13 = bf16[1,800,2048]{2,1,0:T(8,128)(2,1)} copy(bf16[1,800,2048]{2,1,0:T(8,128)(2,1)S(1)} %get-tuple-element.55) | data formatting | bytes 6553600
  (2 shorter events, 0.0 us)

commit v4 on v3

--- a/solution.py
+++ b/solution.py
@@ -115,25 +115,31 @@
     left_lap, left = split(left, peers)
     right_lap, right = split(right, peers)
     together = left_lap == right_lap
+    spans = [slice(device * total, (device + 1) * total) for device in range(peers)]
+    here = [(owner == device).astype(jnp.float32) for device in range(peers)]
+    along = jnp.dot(jnp.concatenate(here, axis=0), before, preferred_element_type=jnp.float32)
+    counts = jnp.zeros(shape, jnp.float32)
+    earlier = []
+    for device in range(peers):
+        counts = jnp.where(lane == device, jnp.sum(here[device], axis=1, keepdims=True), counts)
+        nearer = jnp.where(right < device, right + peers, right) < jnp.where(
+            left < device, left + peers, left
+        )
+        earlier.append((together & nearer).astype(jnp.float32))
+    above = jnp.dot(jnp.concatenate(earlier, axis=0), counts, preferred_element_type=jnp.float32)
     rank = jnp.zeros(shape, jnp.float32)
     for device in range(peers):
-        here = (owner == device).astype(jnp.float32)
-        along = jnp.dot(here, before, preferred_element_type=jnp.float32)
-        nearer = jnp.where(right < device, right + peers, right) < jnp.where(
-            left < device, left + peers, left
-        )
-        earlier = (together & nearer).astype(jnp.float32)
-        above = jnp.dot(earlier, here, preferred_element_type=jnp.float32)
-        above = jnp.sum(above, axis=1, keepdims=True)
-        rank = rank + here * (along + above)
+        ahead = jnp.where(lane == device, above[spans[device]], 0.0)
+        ahead = jnp.sum(ahead, axis=1, keepdims=True)
+        rank = rank + here[device] * (along[spans[device]] + ahead)
     rank = rank.astype(jnp.int32)
     layer, middle = split(rank, peers)
     middle = jnp.where(valid, middle, -1)
+    here = [(middle == device).astype(jnp.float32) for device in range(peers)]
+    along = jnp.dot(jnp.concatenate(here, axis=0), before, preferred_element_type=jnp.float32)
     place = jnp.zeros(shape, jnp.float32)
     for device in range(peers):
-        here = (middle == device).astype(jnp.float32)
-        along = jnp.dot(here, before, preferred_element_type=jnp.float32)
-        place = place + here * along
+        place = place + here[device] * along[spans[device]]
     most = jnp.max(jnp.max(place, axis=1, keepdims=True), axis=0, keepdims=True)
     place = place.astype(jnp.int32)
 

time: 121 us -> 121 us (level)
  no operation moved by 1% of the time
where the time goes in v4:
time: 121 us
  Pallas kernels  118 us (98%)
  local copies, waits for them, and re-layouts  1.71 us (1%)
  between operations  1.32 us (1%)
    pallas_call x1, Pallas kernels, serve(): pl.pallas_call(functools.partial(serve_kernel, peers, held, share), out_s...  106 us
    pallas_call x1, Pallas kernels, find_routes(): pl.pallas_call(functools.partial(route_kernel, groups, peers, held, share...  11.7 us

profile of v4, /device:TPU:15, one launch (start us, length us, event | category | flops | bytes accessed | tf_op | source)
XLA Modules:
  0.0 121.2 jit_solution(3067563618169456794)
XLA Ops:
  0.7 0.4 multiply_sine_fusion
  1.1 11.7 %routes.1 = (s32[8,128]{1,0:T(8,128)S(1)}, s32[1,1]{1,0:T(1,128)}) custom-call(s32[1,64]{1,0:T(1,128)} %row_ref.1), custom_call_target="tpu_custom_call" | custom-call | tf_op jit(solution)/shard_map/routes/pallas_call | solution.py:171
  13.4 106.1 %conditional.1 = (bf16[1,800,2048]{2,1,0:T(8,128)(2,1)S(1)}) conditional(s32[]{:T(128)} %bitcast.12, (s32[1,64]{1,0:T(1,128)}, bf16[64,8,2048]{2,1,0:T(8,128)(2,1)}, s32[1]{0:T(128)}, f32[200,128]{1,0:T(8,128)S(1)}, f32[200,128]{1,0:T(8,128)S(1)}, /*index=5*/bf16[800,2048]{1,0:T(8,128)(2,1)}, bf16[800,2048]{1,0:T(8,128)(2,1)}) %tuple.24, ...), branch_computations={%region_0.4_spmd, %region_4.5_spmd} | conditional | flops 198658 | bytes 46200160 | solution.py:429
  13.6 105.9 %serve.1 = bf16[800,2048]{1,0:T(8,128)(2,1)S(1)} custom-call(s32[8,128]{1,0:T(8,128)S(1)} %get-tuple-element.44.route_ref, s32[1]{0:T(128)} %get-tuple-element.45.length_ref, f32[200,128]{1,0:T(8,128)S(1)} %get-tuple-element.46.cos_ref, f32[200,128]{1,0:T(8,128)S(1)} %get-tuple-element.47.sin_ref, bf16[64,8,2048]{2,1,0:T(8,128)(2,1)} %get-tuple-element.48.store_ref, ...), custom_call_target="tpu_custom_call" | custom-call | tf_op jit(solution)/shard_map/cond/branch_1_fun/serve/pallas_call | solution.py:302
  119.5 1.7 %copy.13 = bf16[1,800,2048]{2,1,0:T(8,128)(2,1)} copy(bf16[1,800,2048]{2,1,0:T(8,128)(2,1)S(1)} %get-tuple-element.55) | data formatting | bytes 6553600
  (2 shorter events, 0.0 us)
